TPU v7x, 32 devices: a whole 2x2x4 slice. The times are simulated.
32 devices in a mesh: ctx: 8 (over z, x), head: 4 (over y, core).
Axes of the slice: x: 2, y: 2, z: 4, core: 2. Of those that a mesh axis runs over, the one named last changes fastest.
Arguments:
- queries: bfloat16 [1024, 4096], P('ctx', 'head'), may hold values from -4 to 4
- keys: bfloat16 [1024, 4096], P('ctx', 'head'), may hold values from -4 to 4
- values: bfloat16 [1024, 4096], P('ctx', 'head'), may hold values from -6 to 6
- outputs: bfloat16 [1024, 4096], P('ctx', 'head'), may hold values from -4 to 4
- grad_out: bfloat16 [1024, 4096], P(('ctx', 'head')), may hold values from -96 to 96
- log_norm: float32 [32, 1024], P('head', 'ctx'), may hold values from 6.5 to 7.5
- glob_keys: bfloat16 [256, 4096], P(None, 'head'), may hold values from -4 to 4
- glob_values: bfloat16 [256, 4096], P(None, 'head'), may hold values from -6 to 6
- key_lists: int32 [8, 6], replicated, may hold values from -1 to 7, as said below
Outputs:
- query_grads: bfloat16 [1024, 4096], P('ctx', 'head')
- key_grads: bfloat16 [1024, 4096], P('ctx', 'head')
- value_grads: bfloat16 [1024, 4096], P('ctx', 'head')
- glob_key_grads: float32 [256, 4096], P('ctx', 'head')
- glob_value_grads: float32 [256, 4096], P('ctx', 'head')
Inputs may be any that keep to these rules, and one draw needn't show every extreme that they name: `key_lists`: row i holds i - 1, i, i + 1 (each -1 where that block lies outside 0 to 7) and then, for r = 1 to 3, one block of group (i + r * 2) mod 8, where group c holds blocks c * 1 to (c + 1) - 1.
All inputs are finite; a program needn't handle non-finite values.
Results may differ from a plain program's by a relative error of at most 0.0055.
Values may be sent and summed in bfloat16 or wider, within the bound.
A program may use at most 64 MiB of HBM per device.

v0:
```python
import functools
import math

import jax
import jax.numpy as jnp
from jax import lax
from jax.experimental import pallas as pl
from jax.experimental.pallas import tpu as pltpu
from jax.sharding import PartitionSpec as P

HEAD_DIM = 128
BLOCK = 128
GLOB = 256
RAND = 3
LOG2E = math.log2(math.e)


def extended_2(cells, sides, width):
    for axis, dim in sides:
        count = lax.axis_size(axis)
        ends = count - 1
        head = lax.slice_in_dim(cells, 0, width, axis=dim)
        tail = lax.slice_in_dim(cells, cells.shape[dim] - width, cells.shape[dim], axis=dim)
        cells = jnp.concatenate(
            [
                lax.ppermute(tail, axis, [(i, (i + 1) % count) for i in range(ends)]),
                cells,
                lax.ppermute(head, axis, [((i + 1) % count, i) for i in range(ends)]),
            ],
            axis=dim,
        )
    return cells


def passed_along(value, axis, by):
    peers = lax.axis_size(axis)
    pairs = [(i, i + by) for i in range(peers) if 0 <= i + by < peers]
    return lax.ppermute(value, axis, pairs)


def shifted(value, axis, by):
    peers = lax.axis_size(axis)
    return lax.ppermute(value, axis, [(i, (i + by) % peers) for i in range(peers)])


def tile_grads(query_rows, grad_rows, norm_rows, delta_rows, key_rows, value_rows, keep_mask):
    att_scale = HEAD_DIM ** (-0.5)
    scores = (
        jnp.einsum("nbd,nkd->nbk", query_rows, key_rows, preferred_element_type=jnp.float32)
        * att_scale
    )
    weights = jnp.exp(scores - norm_rows[:, :, None]) * keep_mask[:, None, :]
    dprobs = jnp.einsum("nbd,nkd->nbk", grad_rows, value_rows, preferred_element_type=jnp.float32)
    dscores = weights * (dprobs - delta_rows[:, :, None])
    weights_low = weights.astype(jnp.bfloat16)
    dscores_low = dscores.astype(jnp.bfloat16)
    grad_values = jnp.einsum(
        "nbk,nbd->nkd", weights_low, grad_rows, preferred_element_type=jnp.float32
    )
    grad_keys = (
        jnp.einsum("nbk,nbd->nkd", dscores_low, query_rows, preferred_element_type=jnp.float32)
        * att_scale
    )
    grad_queries = (
        jnp.einsum("nbk,nkd->nbd", dscores_low, key_rows, preferred_element_type=jnp.float32)
        * att_scale
    )
    return (grad_queries, grad_keys, grad_values)


def head_cols(source, head_index):
    return source[:, head_index * HEAD_DIM : (head_index + 1) * HEAD_DIM]


def head_blocks(source, head_index, num_blocks):
    return head_cols(source, head_index).reshape(num_blocks, BLOCK, HEAD_DIM)


def gather_tiles(tile_rows, slot_ids):
    picked = jnp.take(tile_rows, slot_ids, axis=0)
    return picked.reshape(slot_ids.shape[0], slot_ids.shape[1] * BLOCK, HEAD_DIM)


def tile_picker(slot_ids, hit_mask, num_blocks):
    one_hot = (
        slot_ids[:, :, None] == jnp.arange(num_blocks, dtype=jnp.int32)[None, None, :]
    ) & hit_mask[:, :, None]
    return one_hot.astype(jnp.float32)


def add_tiles(picker, flat_grads, num_blocks):
    tiled_grads = flat_grads.reshape(picker.shape[0], picker.shape[1], BLOCK, HEAD_DIM)
    summed = jnp.einsum("nle,nlbd->ebd", picker, tiled_grads, precision=lax.Precision.HIGHEST)
    return summed.reshape(num_blocks * BLOCK, HEAD_DIM)


def tile_keep(hit_mask, extra_cols):
    tile_cols = jnp.repeat(hit_mask.astype(jnp.float32), BLOCK, axis=1)
    return jnp.concatenate(
        [jnp.ones((hit_mask.shape[0], extra_cols), jnp.float32), tile_cols], axis=1
    )


def with_glob(glob_rows, tile_rows):
    spread = glob_rows[None]
    return jnp.concatenate([spread, tile_rows], axis=1)


def shards(queries, keys, values, outputs, grad_out, log_norm, glob_keys, glob_values, key_lists):
    row_count, col_count = queries.shape
    head_count = col_count // HEAD_DIM
    block_count = row_count // BLOCK
    group_count = lax.axis_size("ctx")
    my_group = lax.axis_index("ctx")
    first_block = my_group * block_count
    incoming = lax.all_to_all(grad_out, "head", split_axis=1, concat_axis=0, tiled=True)
    row_delta = jnp.sum(
        (incoming.astype(jnp.float32) * outputs.astype(jnp.float32)).reshape(
            row_count, head_count, HEAD_DIM
        ),
        axis=2,
    ).T
    own_lists = lax.dynamic_slice_in_dim(key_lists, first_block, block_count, 0)
    query_heads = [
        head_blocks(queries, head_index, block_count) for head_index in range(head_count)
    ]
    grad_heads = [
        head_blocks(incoming, head_index, block_count) for head_index in range(head_count)
    ]
    norm_heads = [
        log_norm[head_index].reshape(block_count, BLOCK) for head_index in range(head_count)
    ]
    delta_heads = [
        row_delta[head_index].reshape(block_count, BLOCK) for head_index in range(head_count)
    ]
    extended = extended_2(jnp.stack([keys, values]), (("ctx", 1),), BLOCK)
    ext_blocks = block_count + 2
    near_lists = own_lists[:, :3]
    near_live = near_lists >= 0
    near_slots = jnp.clip(near_lists - (first_block - 1), 0, ext_blocks - 1)
    near_keep = tile_keep(near_live, GLOB)
    near_picker = tile_picker(near_slots, near_live, ext_blocks)
    dq_parts, dk_parts, dv_parts, glob_dk_parts, glob_dv_parts = ([], [], [], [], [])
    for head_index in range(head_count):
        ext_keys = head_blocks(extended[0], head_index, ext_blocks)
        ext_values = head_blocks(extended[1], head_index, ext_blocks)
        key_rows = with_glob(head_cols(glob_keys, head_index), gather_tiles(ext_keys, near_slots))
        value_rows = with_glob(
            head_cols(glob_values, head_index), gather_tiles(ext_values, near_slots)
        )
        grad_q, grad_k, grad_v = tile_grads(
            query_heads[head_index],
            grad_heads[head_index],
            norm_heads[head_index],
            delta_heads[head_index],
            key_rows,
            value_rows,
            near_keep,
        )
        dq_parts.append(grad_q.reshape(row_count, HEAD_DIM))
        glob_dk_parts.append(jnp.sum(grad_k[:, :GLOB], axis=0))
        glob_dv_parts.append(jnp.sum(grad_v[:, :GLOB], axis=0))
        dk_parts.append(add_tiles(near_picker, grad_k[:, GLOB:], ext_blocks))
        dv_parts.append(add_tiles(near_picker, grad_v[:, GLOB:], ext_blocks))
    query_side = jnp.concatenate(dq_parts, axis=1)
    near_side = jnp.stack([jnp.concatenate(dk_parts, axis=1), jnp.concatenate(dv_parts, axis=1)])
    own_grads = near_side[:, BLOCK : BLOCK + row_count]
    for shift_by in (-1, 1):
        rim_piece = near_side[:, :BLOCK] if shift_by < 0 else near_side[:, BLOCK + row_count :]
        arrived = passed_along(rim_piece, "ctx", shift_by)
        if shift_by < 0:
            own_grads = own_grads.at[:, row_count - BLOCK :].add(arrived)
        else:
            own_grads = own_grads.at[:, :BLOCK].add(arrived)
    full_keep = jnp.ones((block_count, BLOCK), jnp.float32)
    all_hit = jnp.ones((block_count, 1), bool)
    own_pair = jnp.stack([keys, values])
    for round_index in range(RAND):
        hop = (round_index + 1) * group_count // (RAND + 1)
        fetched = shifted(own_pair, "ctx", -hop)
        target_first = (my_group + hop) % group_count * block_count
        far_slots = jnp.clip(own_lists[:, 3 + round_index] - target_first, 0, block_count - 1)[
            :, None
        ]
        far_picker = tile_picker(far_slots, all_hit, block_count)
        far_dq, far_dk, far_dv = ([], [], [])
        for head_index in range(head_count):
            far_keys = gather_tiles(head_blocks(fetched[0], head_index, block_count), far_slots)
            far_values = gather_tiles(head_blocks(fetched[1], head_index, block_count), far_slots)
            grad_q, grad_k, grad_v = tile_grads(
                query_heads[head_index],
                grad_heads[head_index],
                norm_heads[head_index],
                delta_heads[head_index],
                far_keys,
                far_values,
                full_keep,
            )
            far_dq.append(grad_q.reshape(row_count, HEAD_DIM))
            far_dk.append(add_tiles(far_picker, grad_k, block_count))
            far_dv.append(add_tiles(far_picker, grad_v, block_count))
        query_side = query_side + jnp.concatenate(far_dq, axis=1)
        far_pair = jnp.stack([jnp.concatenate(far_dk, axis=1), jnp.concatenate(far_dv, axis=1)])
        own_grads = own_grads + shifted(far_pair, "ctx", hop)
    glob_pair = jnp.stack(
        [jnp.concatenate(glob_dk_parts, axis=1), jnp.concatenate(glob_dv_parts, axis=1)]
    )
    summed_all = lax.psum(glob_pair, "ctx")
    share_rows = GLOB // group_count
    own_share = lax.dynamic_slice_in_dim(summed_all, my_group * share_rows, share_rows, 1)
    return (
        query_side.astype(jnp.bfloat16),
        own_grads[0].astype(jnp.bfloat16),
        own_grads[1].astype(jnp.bfloat16),
        own_share[0],
        own_share[1],
    )


HALVES = 2
HALF = BLOCK // HALVES
K_IN, V_IN, S_IN, Q_IN, G_IN = 0, 1, 2, 3, 3 + HALVES
IN_KINDS = 3 + 2 * HALVES
K_OUT, V_OUT, GLOB_OUT, Q_OUT = 0, 1, 2, 3
OUT_KINDS = 3 + HALVES
CLASSES = 2
CONTRACT_LAST = (((1,), (1,)), ((), ()))


def start_order(peers):
    half = peers // 2
    return [half] + [half + sign * by for by in range(1, half) for sign in (-1, 1)]


def head_kernel(
    peers,
    q_hbm,
    k_hbm,
    v_hbm,
    o_hbm,
    g_hbm,
    norm_hbm,
    gk_hbm,
    gv_hbm,
    dq_hbm,
    dk_hbm,
    dv_hbm,
    glob_hbm,
    q_own,
    k_own,
    v_own,
    g_part,
    dq_out,
    dk_out,
    dv_out,
    glob_out,
    q_all,
    k_all,
    v_all,
    g_all,
    stat_all,
    g_own,
    o_own,
    norm_own,
    stat_own,
    kt_all,
    dq_acc,
    dk_acc,
    dv_acc,
    dq_low,
    dk_low,
    dv_low,
    glob_low,
    load_sem,
    spread_send,
    spread_recv,
    in_send,
    in_recv,
    out_send,
    out_recv,
):
    me = lax.axis_index("ctx")
    my_head = lax.axis_index("head")
    head_peers = lax.axis_size("head")
    members = peers // CLASSES
    class_rows = members * BLOCK
    span = class_rows + GLOB
    share = GLOB // peers
    width = q_hbm.shape[1]
    part_rows = g_part.shape[0]
    order = start_order(peers)

    def cols(index):
        return pl.ds(pl.multiple_of(index * HEAD_DIM, HEAD_DIM), HEAD_DIM)

    def query_rows(half, index):
        at = half * members * CLASSES * HALF + (index % CLASSES) * members * HALF + (index // CLASSES) * HALF
        return pl.ds(at if isinstance(at, int) else pl.multiple_of(at, HALF), HALF)

    def half_rows(half):
        return pl.ds(half * HALF, HALF)

    def key_rows(index):
        at = (index % CLASSES) * span + (index // CLASSES) * BLOCK
        return pl.ds(at if isinstance(at, int) else pl.multiple_of(at, BLOCK), BLOCK)

    def remote(src, dst, send, recv, **device):
        return pltpu.make_async_remote_copy(
            src_ref=src,
            dst_ref=dst,
            send_sem=send,
            recv_sem=recv,
            device_id=device,
            device_id_type=pl.DeviceIdType.MESH,
        )

    loads = [
        pltpu.make_async_copy(o_hbm, o_own, load_sem.at[0]),
        pltpu.make_async_copy(norm_hbm, norm_own, load_sem.at[1]),
        pltpu.make_async_copy(
            gk_hbm.at[:, cols(me)], k_all.at[pl.ds(class_rows, GLOB)], load_sem.at[2]
        ),
        pltpu.make_async_copy(
            gv_hbm.at[:, cols(me)], v_all.at[pl.ds(class_rows, GLOB)], load_sem.at[3]
        ),
    ]
    firsts = [
        pltpu.make_async_copy(src, dst, load_sem.at[4 + at])
        for at, (src, dst) in enumerate(
            ((g_hbm, g_part), (k_hbm, k_own), (q_hbm, q_own), (v_hbm, v_own))
        )
    ]
    for load in firsts:
        load.start()
    for load in loads:
        load.start()

    barrier = pltpu.get_barrier_semaphore()
    for by in range(1, head_peers):
        pl.semaphore_signal(
            barrier,
            inc=1,
            device_id={"head": lax.rem(my_head + by, head_peers)},
            device_id_type=pl.DeviceIdType.MESH,
        )
    for by in order:
        pl.semaphore_signal(
            barrier,
            inc=1,
            device_id={"ctx": lax.rem(me + by, peers)},
            device_id_type=pl.DeviceIdType.MESH,
        )
    pl.semaphore_wait(barrier, head_peers - 1 + peers - 1)

    sends = []
    firsts[0].wait()

    def my_part():
        return pl.ds(pl.multiple_of(my_head * part_rows, part_rows), part_rows)

    def wide(index):
        return pl.ds(pl.multiple_of(index * width, width), width)

    for by in range(1, head_peers):
        to = lax.rem(my_head + by, head_peers)
        copy = remote(
            g_part.at[:, wide(to)],
            g_own.at[my_part()],
            spread_send.at[by],
            spread_recv.at[my_head],
            head=to,
        )
        copy.start()
        sends.append(copy)
    pltpu.make_async_copy(
        g_part.at[:, wide(my_head)], g_own.at[my_part()], spread_recv.at[my_head]
    ).start()

    def spread_in(kind, src, dst, from_rows, rows):
        for by in order:
            to = lax.rem(me + by, peers)
            copy = remote(
                src.at[from_rows, cols(to)],
                dst.at[rows(me)],
                in_send.at[kind, by],
                in_recv.at[kind, me],
                ctx=to,
            )
            copy.start()
            sends.append(copy)
        pltpu.make_async_copy(
            src.at[from_rows, cols(me)], dst.at[rows(me)], in_recv.at[kind, me]
        ).start()

    def arrived(kind, dst, rows):
        for index in range(peers):
            place = dst.at[rows(index)]
            pltpu.make_async_copy(place, place, in_recv.at[kind, index]).wait()

    places = [functools.partial(query_rows, half) for half in range(HALVES)]
    all_rows = pl.ds(0, BLOCK)
    firsts[1].wait()
    spread_in(K_IN, k_own, k_all, all_rows, key_rows)
    firsts[2].wait()
    spread_in(Q_IN, q_own, q_all, half_rows(0), places[0])
    firsts[3].wait()
    spread_in(V_IN, v_own, v_all, all_rows, key_rows)

    loads[0].wait()
    loads[1].wait()
    for index in range(head_peers):
        place = g_own.at[pl.ds(index * part_rows, part_rows)]
        pltpu.make_async_copy(place, place, spread_recv.at[index]).wait()
    spread_in(G_IN, g_own, g_all, half_rows(0), places[0])
    ones = jnp.ones((8, HEAD_DIM), jnp.float32)
    first = lax.broadcasted_iota(jnp.int32, (8, BLOCK), 0) == 0
    for index in range(peers):
        lanes = pl.ds(index * HEAD_DIM, HEAD_DIM)
        product = g_own[:, lanes].astype(jnp.float32) * o_own[:, lanes].astype(jnp.float32)
        delta = lax.dot_general(
            ones,
            product,
            CONTRACT_LAST,
            precision=lax.Precision.HIGHEST,
            preferred_element_type=jnp.float32,
        )
        norm = jnp.broadcast_to(norm_own[pl.ds(index, 1), :], (8, BLOCK))
        stat_own[index] = jnp.where(first, norm * LOG2E, delta)
    for by in order:
        to = lax.rem(me + by, peers)
        copy = remote(
            stat_own.at[to], stat_all.at[me], in_send.at[S_IN, by], in_recv.at[S_IN, me], ctx=to
        )
        copy.start()
        sends.append(copy)
    pltpu.make_async_copy(stat_own.at[me], stat_all.at[me], in_recv.at[S_IN, me]).start()

    for half in range(1, HALVES):
        spread_in(Q_IN + half, q_own, q_all, half_rows(half), places[half])
        spread_in(G_IN + half, g_own, g_all, half_rows(half), places[half])

    scale = HEAD_DIM**-0.5

    def dot(left, right):
        return jnp.dot(left, right, preferred_element_type=jnp.float32)

    def visit(half, blocks, key_at, key_count, keep):
        rows = pl.ds(query_rows(half, blocks[0]).start, len(blocks) * HALF)
        keys = pl.ds(key_at, key_count)
        norm, delta = (
            jnp.concatenate(
                [stat_all[block, row : row + 1, half * HALF : (half + 1) * HALF] for block in blocks],
                axis=1,
            )
            for row in range(2)
        )
        scores = lax.dot_general(
            k_all[keys, :], q_all[rows, :], CONTRACT_LAST, preferred_element_type=jnp.float32
        )
        weights = jnp.exp2(scores * (scale * LOG2E) - norm)
        if keep is not None:
            weights = jnp.where(keep, weights, 0.0)
        dprobs = lax.dot_general(
            v_all[keys, :], g_all[rows, :], CONTRACT_LAST, preferred_element_type=jnp.float32
        )
        dscores = (weights * (dprobs - delta)).astype(jnp.bfloat16)
        dq_acc[:, rows] += dot(kt_all[:, keys], dscores)
        dk_acc[keys, :] += dot(dscores, q_all[rows, :])
        dv_acc[keys, :] += dot(weights.astype(jnp.bfloat16), g_all[rows, :])

    def visit_near(half, blocks):
        near = [at for at in range(blocks[0] - 1, blocks[-1] + 2, CLASSES) if 0 <= at < peers]
        shape = (len(near) * BLOCK, len(blocks) * HALF)
        key_block = near[0] + CLASSES * (lax.broadcasted_iota(jnp.int32, shape, 0) // BLOCK)
        query_block = blocks[0] + CLASSES * (lax.broadcasted_iota(jnp.int32, shape, 1) // HALF)
        keep = jnp.abs(key_block - query_block) == 1
        visit(half, blocks, key_rows(near[0]).start, len(near) * BLOCK, keep)

    def put(kind, src, dst, from_rows, to_rows, block):
        @pl.when(me == block)
        def _():
            pltpu.make_async_copy(
                src.at[from_rows], dst.at[to_rows, cols(me)], out_recv.at[kind, me]
            ).start()

        @pl.when(me != block)
        def _():
            remote(
                src.at[from_rows],
                dst.at[to_rows, cols(me)],
                out_send.at[kind, block],
                out_recv.at[kind, me],
                ctx=block,
            ).start()

    dk_acc[...] = jnp.zeros_like(dk_acc)
    dv_acc[...] = jnp.zeros_like(dv_acc)
    dq_acc[...] = jnp.zeros_like(dq_acc)

    loads[2].wait()
    loads[3].wait()
    arrived(K_IN, k_all, key_rows)
    kt_all[...] = k_all[...].T
    arrived(V_IN, v_all, key_rows)
    for index in range(peers):
        place = stat_all.at[index]
        pltpu.make_async_copy(place, place, in_recv.at[S_IN, index]).wait()

    pair = 2
    for half in range(HALVES):
        arrived(Q_IN + half, q_all, places[half])
        arrived(G_IN + half, g_all, places[half])
        for part in range(CLASSES):
            for at in range(0, members, pair):
                visit_near(half, [part + CLASSES * (at + step) for step in range(pair)])
        for part in range(CLASSES):
            blocks = [part + CLASSES * at for at in range(members)]
            visit(half, blocks, part * class_rows, span, None)
            rows = pl.ds(query_rows(half, part).start, members * HALF)
            dq_low[rows, :] = (dq_acc[:, rows] * scale).T.astype(jnp.bfloat16)
            for block in blocks:
                put(Q_OUT + half, dq_low, dq_out, query_rows(half, block), half_rows(half), block)
            if half == HALVES - 1:
                own = pl.ds(part * span, class_rows)
                dk_low[own, :] = (dk_acc[own, :] * scale).astype(jnp.bfloat16)
                for block in blocks:
                    put(K_OUT, dk_low, dk_out, key_rows(block), all_rows, block)
                dv_low[own, :] = dv_acc[own, :].astype(jnp.bfloat16)
                for block in blocks:
                    put(V_OUT, dv_low, dv_out, key_rows(block), all_rows, block)

    middle = pl.ds(class_rows, GLOB)
    glob_low[0] = (dk_acc[middle, :] * scale).astype(jnp.bfloat16)
    glob_low[1] = dv_acc[middle, :].astype(jnp.bfloat16)

    def share_of(index):
        return glob_low.at[:, pl.ds(pl.multiple_of(index * share, share), share), :]

    for by in order:
        to = lax.rem(me + by, peers)
        copy = remote(
            share_of(to),
            glob_out.at[:, :, cols(me)],
            out_send.at[GLOB_OUT, to],
            out_recv.at[GLOB_OUT, me],
            ctx=to,
        )
        copy.start()
        sends.append(copy)
    pltpu.make_async_copy(
        share_of(me), glob_out.at[:, :, cols(me)], out_recv.at[GLOB_OUT, me]
    ).start()

    stores = []

    def store(at, src, dst):
        copy = pltpu.make_async_copy(src, dst, load_sem.at[8 + at])
        copy.start()
        stores.append(copy)

    for half in range(HALVES):
        for index in range(peers):
            place = dq_out.at[half_rows(half), cols(index)]
            pltpu.make_async_copy(place, place, out_recv.at[Q_OUT + half, index]).wait()
    store(0, dq_out, dq_hbm)
    for at, (kind, dst, home) in enumerate(((K_OUT, dk_out, dk_hbm), (V_OUT, dv_out, dv_hbm))):
        for index in range(peers):
            place = dst.at[:, cols(index)]
            pltpu.make_async_copy(place, place, out_recv.at[kind, index]).wait()
        store(1 + at, dst, home)
    for index in range(peers):
        place = glob_out.at[:, :, cols(index)]
        pltpu.make_async_copy(place, place, out_recv.at[GLOB_OUT, index]).wait()
    store(3, glob_out, glob_hbm)

    for copy in sends:
        copy.wait_send()
    halves = [(Q_OUT + half, dq_low, places[half]) for half in range(HALVES)]
    for by in order:
        to = lax.rem(me + by, peers)
        for kind, src, rows in [(K_OUT, dk_low, key_rows), (V_OUT, dv_low, key_rows)] + halves:
            place = src.at[rows(to)]
            pltpu.make_async_copy(place, place, out_send.at[kind, to]).wait()
    for copy in stores:
        copy.wait()


def finish_kernel(
    dq_in, dk_in, dv_in, glob_in, dq_out, dk_out, dv_out, gk_out, gv_out, held, low, wide, load, save
):
    loads = [
        pltpu.make_async_copy(src, dst, load.at[at])
        for at, (src, dst) in enumerate(
            ((glob_in, low), (dq_in, held.at[0]), (dk_in, held.at[1]), (dv_in, held.at[2]))
        )
    ]
    for copy in loads:
        copy.start()
    saves = [
        pltpu.make_async_copy(src, dst, save.at[at])
        for at, (src, dst) in enumerate(
            (
                (wide.at[0], gk_out),
                (wide.at[1], gv_out),
                (held.at[0], dq_out),
                (held.at[1], dk_out),
                (held.at[2], dv_out),
            )
        )
    ]
    loads[0].wait()
    wide[...] = low[...].astype(jnp.float32)
    saves[0].start()
    saves[1].start()
    for ready, copy in zip(loads[1:], saves[2:]):
        ready.wait()
        copy.start()
    for copy in saves:
        copy.wait()


def whole_heads(peers, queries, keys, values, outputs, grad_out, log_norm, glob_keys, glob_values):
    row_count, col_count = queries.shape
    tokens = peers * BLOCK
    low, full = jnp.bfloat16, jnp.float32
    head_peers = lax.axis_size("head")
    result = jax.ShapeDtypeStruct((row_count, col_count), low)
    scores = tokens * (GLOB + (RAND + 3) * BLOCK)
    dq, dk, dv, glob = pl.pallas_call(
        functools.partial(head_kernel, peers),
        out_shape=(
            result,
            result,
            result,
            jax.ShapeDtypeStruct((2, GLOB // peers, col_count), low),
        ),
        in_specs=[pl.BlockSpec(memory_space=pl.ANY)] * 8,
        out_specs=[pl.BlockSpec(memory_space=pl.ANY)] * 4,
        scratch_shapes=[
            pltpu.VMEM((row_count, col_count), low),
            pltpu.VMEM((row_count, col_count), low),
            pltpu.VMEM((row_count, col_count), low),
            pltpu.VMEM(grad_out.shape, low),
            pltpu.VMEM((row_count, col_count), low),
            pltpu.VMEM((row_count, col_count), low),
            pltpu.VMEM((row_count, col_count), low),
            pltpu.VMEM((2, GLOB // peers, col_count), low),
            pltpu.VMEM((tokens, HEAD_DIM), low),
            pltpu.VMEM((tokens + GLOB, HEAD_DIM), low),
            pltpu.VMEM((tokens + GLOB, HEAD_DIM), low),
            pltpu.VMEM((tokens, HEAD_DIM), low),
            pltpu.VMEM((peers, 8, BLOCK), full),
            pltpu.VMEM((row_count, col_count), low),
            pltpu.VMEM((row_count, col_count), low),
            pltpu.VMEM(log_norm.shape, full),
            pltpu.VMEM((peers, 8, BLOCK), full),
            pltpu.VMEM((HEAD_DIM, tokens + GLOB), low),
            pltpu.VMEM((HEAD_DIM, tokens), full),
            pltpu.VMEM((tokens + GLOB, HEAD_DIM), full),
            pltpu.VMEM((tokens + GLOB, HEAD_DIM), full),
            pltpu.VMEM((tokens, HEAD_DIM), low),
            pltpu.VMEM((tokens + GLOB, HEAD_DIM), low),
            pltpu.VMEM((tokens + GLOB, HEAD_DIM), low),
            pltpu.VMEM((2, GLOB, HEAD_DIM), low),
            pltpu.SemaphoreType.DMA((12,)),
            pltpu.SemaphoreType.DMA((head_peers,)),
            pltpu.SemaphoreType.DMA((head_peers,)),
            pltpu.SemaphoreType.DMA((IN_KINDS, peers)),
            pltpu.SemaphoreType.DMA((IN_KINDS, peers)),
            pltpu.SemaphoreType.DMA((OUT_KINDS, peers)),
            pltpu.SemaphoreType.DMA((OUT_KINDS, peers)),
        ],
        compiler_params=pltpu.CompilerParams(
            collective_id=0, has_side_effects=True, vmem_limit_bytes=64 * 1024 * 1024
        ),
        cost_estimate=pl.CostEstimate(
            flops=10 * scores * HEAD_DIM, bytes_accessed=4 * 1024 * 1024, transcendentals=scores
        ),
        name="whole_heads",
    )(queries, keys, values, outputs, grad_out, log_norm, glob_keys, glob_values)
    share = jax.ShapeDtypeStruct((GLOB // peers, col_count), full)
    hbm = pl.BlockSpec(memory_space=pltpu.HBM)
    return pl.pallas_call(
        finish_kernel,
        out_shape=(result, result, result, share, share),
        in_specs=[pl.BlockSpec(memory_space=pl.ANY)] * 4,
        out_specs=[hbm] * 5,
        scratch_shapes=[
            pltpu.VMEM((3, row_count, col_count), low),
            pltpu.VMEM((2, GLOB // peers, col_count), low),
            pltpu.VMEM((2, GLOB // peers, col_count), full),
            pltpu.SemaphoreType.DMA((4,)),
            pltpu.SemaphoreType.DMA((5,)),
        ],
        compiler_params=pltpu.CompilerParams(vmem_limit_bytes=64 * 1024 * 1024),
        cost_estimate=pl.CostEstimate(
            flops=0, bytes_accessed=2 * 1024 * 1024, transcendentals=0
        ),
        name="finish",
    )(dq, dk, dv, glob)


def program(mesh):
    peers = mesh.shape["ctx"]

    def body(queries, keys, values, outputs, grad_out, log_norm, glob_keys, glob_values, key_lists):
        row_count, col_count = queries.shape
        one_head_each = (
            row_count == BLOCK
            and col_count == peers * HEAD_DIM
            and peers == CLASSES * (RAND + 1)
            and GLOB % (16 * peers) == 0
        )
        if one_head_each:
            return whole_heads(
                peers, queries, keys, values, outputs, grad_out, log_norm, glob_keys, glob_values
            )
        return shards(
            queries, keys, values, outputs, grad_out, log_norm, glob_keys, glob_values, key_lists
        )

    return body


def solution(mesh):
    in_specs = (
        P("ctx", "head"),
        P("ctx", "head"),
        P("ctx", "head"),
        P("ctx", "head"),
        P(("ctx", "head"), None),
        P("head", "ctx"),
        P(None, "head"),
        P(None, "head"),
        P(),
    )
    out_specs = (
        P("ctx", "head"),
        P("ctx", "head"),
        P("ctx", "head"),
        P("ctx", "head"),
        P("ctx", "head"),
    )
    return jax.shard_map(program(mesh), mesh=mesh, in_specs=in_specs, out_specs=out_specs, check_vma=False)
```

profile of v0, /device:TPU:0, one launch (start us, length us, event | category | flops | bytes accessed | tf_op | source)
XLA Modules:
  0.0 56.5 jit_solution(2616817058337073718)
XLA Ops:
  0.6 53.9 %whole_heads.1 = (bf16[128,1024]{1,0:T(8,128)(2,1)}, bf16[128,1024]{1,0:T(8,128)(2,1)}, bf16[128,1024]{1,0:T(8,128)(2,1)}, bf16[2,32,1024]{2,1,0:T(8,128)(2,1)}) custom-call(bf16[128,1024]{1,0:T(8,128)(2,1)} %q_hbm.1, bf16[128,1024]{1,0:T(8,128)(2,1)} %k_hbm.1, bf16[128,1024]{1,0:T(8,128)(2,1)} %v_hbm.1, bf16[128,1024]{1,0:T(8,128)(2,1)} %o_hbm.1, ...), custom_call_target="tpu_custom_call" | custom-call | flops 1342177280 | bytes 4194304 | tf_op jit(solution)/shard_map/whole_heads/pallas_call | solution.py:629
  54.5 2.0 %finish.1 = (bf16[128,1024]{1,0:T(8,128)(2,1)}, bf16[128,1024]{1,0:T(8,128)(2,1)}, bf16[128,1024]{1,0:T(8,128)(2,1)}, f32[32,1024]{1,0:T(8,128)}, f32[32,1024]{1,0:T(8,128)}) custom-call(bf16[128,1024]{1,0:T(8,128)(2,1)} %get-tuple-element.9.dq_in, bf16[128,1024]{1,0:T(8,128)(2,1)} %get-tuple-element.10.dk_in, bf16[128,1024]{1,0:T(8,128)(2,1)} %get-tuple-element.11.dv_in, ...), custom_call_target="tpu_custom_call" | custom-call | bytes 2097152 | tf_op jit(solution)/shard_map/finish/pallas_call | solution.py:683
where the time goes:
time: 56.6 us; the launch traced here: 56.5 us
  Pallas kernels  55.8 us (99%)
  between operations  0.64 us (1%)
    pallas_call x1, Pallas kernels, whole_heads(): pl.pallas_call(functools.partial(head_kernel, peers), out_shape=(result,...  53.9 us
    pallas_call x1, Pallas kernels, whole_heads(): pl.pallas_call(finish_kernel, out_shape=(result, result, result, share, s...  1.97 us

commit v1 on v0

--- a/solution.py
+++ b/solution.py
@@ -219,8 +219,9 @@
 
 HALVES = 2
 HALF = BLOCK // HALVES
-K_IN, V_IN, S_IN, Q_IN, G_IN = 0, 1, 2, 3, 3 + HALVES
-IN_KINDS = 3 + 2 * HALVES
+K_IN, V_IN, NORM_IN, DELTA_IN, Q_IN, G_IN = 0, 1, 2, 3, 4, 4 + HALVES
+IN_KINDS = 4 + 2 * HALVES
+PAIR = 2
 K_OUT, V_OUT, GLOB_OUT, Q_OUT = 0, 1, 2, 3
 OUT_KINDS = 3 + HALVES
 CLASSES = 2
@@ -258,12 +259,18 @@
     k_all,
     v_all,
     g_all,
-    stat_all,
+    norm_all,
+    delta_all,
     g_own,
     o_own,
     norm_own,
-    stat_own,
+    norm_tiles,
+    delta_tiles,
     kt_all,
+    far_weights,
+    far_low,
+    near_weights,
+    near_low,
     dq_acc,
     dk_acc,
     dv_acc,
@@ -399,44 +406,53 @@
 
     places = [functools.partial(query_rows, half) for half in range(HALVES)]
     all_rows = pl.ds(0, BLOCK)
+    def tiles_in(kind, src, dst):
+        for by in order:
+            to = lax.rem(me + by, peers)
+            copy = remote(
+                src.at[to], dst.at[me], in_send.at[kind, by], in_recv.at[kind, me], ctx=to
+            )
+            copy.start()
+            sends.append(copy)
+        pltpu.make_async_copy(src.at[me], dst.at[me], in_recv.at[kind, me]).start()
+
+    def tiles_arrived(kind, dst):
+        for index in range(peers):
+            place = dst.at[index]
+            pltpu.make_async_copy(place, place, in_recv.at[kind, index]).wait()
+
     firsts[1].wait()
     spread_in(K_IN, k_own, k_all, all_rows, key_rows)
     firsts[2].wait()
     spread_in(Q_IN, q_own, q_all, half_rows(0), places[0])
+    loads[1].wait()
+    for index in range(peers):
+        norm = norm_own[pl.ds(index, 1), :] * LOG2E
+        norm_tiles[index] = jnp.broadcast_to(norm, (8, BLOCK))
+    tiles_in(NORM_IN, norm_tiles, norm_all)
+    for half in range(1, HALVES):
+        spread_in(Q_IN + half, q_own, q_all, half_rows(half), places[half])
     firsts[3].wait()
     spread_in(V_IN, v_own, v_all, all_rows, key_rows)
 
     loads[0].wait()
-    loads[1].wait()
     for index in range(head_peers):
         place = g_own.at[pl.ds(index * part_rows, part_rows)]
         pltpu.make_async_copy(place, place, spread_recv.at[index]).wait()
     spread_in(G_IN, g_own, g_all, half_rows(0), places[0])
     ones = jnp.ones((8, HEAD_DIM), jnp.float32)
-    first = lax.broadcasted_iota(jnp.int32, (8, BLOCK), 0) == 0
     for index in range(peers):
         lanes = pl.ds(index * HEAD_DIM, HEAD_DIM)
         product = g_own[:, lanes].astype(jnp.float32) * o_own[:, lanes].astype(jnp.float32)
-        delta = lax.dot_general(
+        delta_tiles[index] = lax.dot_general(
             ones,
             product,
             CONTRACT_LAST,
             precision=lax.Precision.HIGHEST,
             preferred_element_type=jnp.float32,
         )
-        norm = jnp.broadcast_to(norm_own[pl.ds(index, 1), :], (8, BLOCK))
-        stat_own[index] = jnp.where(first, norm * LOG2E, delta)
-    for by in order:
-        to = lax.rem(me + by, peers)
-        copy = remote(
-            stat_own.at[to], stat_all.at[me], in_send.at[S_IN, by], in_recv.at[S_IN, me], ctx=to
-        )
-        copy.start()
-        sends.append(copy)
-    pltpu.make_async_copy(stat_own.at[me], stat_all.at[me], in_recv.at[S_IN, me]).start()
-
+    tiles_in(DELTA_IN, delta_tiles, delta_all)
     for half in range(1, HALVES):
-        spread_in(Q_IN + half, q_own, q_all, half_rows(half), places[half])
         spread_in(G_IN + half, g_own, g_all, half_rows(half), places[half])
 
     scale = HEAD_DIM**-0.5
@@ -444,37 +460,75 @@
     def dot(left, right):
         return jnp.dot(left, right, preferred_element_type=jnp.float32)
 
-    def visit(half, blocks, key_at, key_count, keep):
-        rows = pl.ds(query_rows(half, blocks[0]).start, len(blocks) * HALF)
+    def row_of(tiles, half, blocks):
+        return jnp.concatenate(
+            [tiles[block, 0:1, half * HALF : (half + 1) * HALF] for block in blocks], axis=1
+        )
+
+    def rows_of(half, blocks):
+        return pl.ds(query_rows(half, blocks[0]).start, len(blocks) * HALF)
+
+    def weigh(half, blocks, key_at, key_count, keep, full, low):
+        rows = rows_of(half, blocks)
         keys = pl.ds(key_at, key_count)
-        norm, delta = (
-            jnp.concatenate(
-                [stat_all[block, row : row + 1, half * HALF : (half + 1) * HALF] for block in blocks],
-                axis=1,
-            )
-            for row in range(2)
-        )
         scores = lax.dot_general(
             k_all[keys, :], q_all[rows, :], CONTRACT_LAST, preferred_element_type=jnp.float32
         )
-        weights = jnp.exp2(scores * (scale * LOG2E) - norm)
+        weights = jnp.exp2(scores * (scale * LOG2E) - row_of(norm_all, half, blocks))
         if keep is not None:
             weights = jnp.where(keep, weights, 0.0)
+        full[pl.ds(0, key_count), :] = weights
+        low[pl.ds(0, key_count), :] = weights.astype(jnp.bfloat16)
+
+    def push(half, blocks, key_at, key_count, full, low):
+        rows = rows_of(half, blocks)
+        keys = pl.ds(key_at, key_count)
         dprobs = lax.dot_general(
             v_all[keys, :], g_all[rows, :], CONTRACT_LAST, preferred_element_type=jnp.float32
         )
-        dscores = (weights * (dprobs - delta)).astype(jnp.bfloat16)
+        weights = full[pl.ds(0, key_count), :]
+        dscores = (weights * (dprobs - row_of(delta_all, half, blocks))).astype(jnp.bfloat16)
+        dv_acc[keys, :] += dot(low[pl.ds(0, key_count), :], g_all[rows, :])
+        dk_acc[keys, :] += dot(dscores, q_all[rows, :])
         dq_acc[:, rows] += dot(kt_all[:, keys], dscores)
-        dk_acc[keys, :] += dot(dscores, q_all[rows, :])
-        dv_acc[keys, :] += dot(weights.astype(jnp.bfloat16), g_all[rows, :])
-
-    def visit_near(half, blocks):
-        near = [at for at in range(blocks[0] - 1, blocks[-1] + 2, CLASSES) if 0 <= at < peers]
+
+    def pairs(part):
+        return [
+            [part + CLASSES * (at + step) for step in range(PAIR)]
+            for at in range(0, members, PAIR)
+        ]
+
+    def near_keys(blocks):
+        return [at for at in range(blocks[0] - 1, blocks[-1] + 2, CLASSES) if 0 <= at < peers]
+
+    def near_slot(half, blocks):
+        part, at = blocks[0] % CLASSES, blocks[0] // CLASSES // PAIR
+        slot = (half * CLASSES + part) * (members // PAIR) + at
+        return near_weights.at[slot], near_low.at[slot]
+
+    def weigh_near(half, blocks):
+        near = near_keys(blocks)
         shape = (len(near) * BLOCK, len(blocks) * HALF)
         key_block = near[0] + CLASSES * (lax.broadcasted_iota(jnp.int32, shape, 0) // BLOCK)
         query_block = blocks[0] + CLASSES * (lax.broadcasted_iota(jnp.int32, shape, 1) // HALF)
         keep = jnp.abs(key_block - query_block) == 1
-        visit(half, blocks, key_rows(near[0]).start, len(near) * BLOCK, keep)
+        at = key_rows(near[0]).start
+        weigh(half, blocks, at, len(near) * BLOCK, keep, *near_slot(half, blocks))
+
+    def push_near(half, part):
+        for blocks in pairs(part):
+            near = near_keys(blocks)
+            at = key_rows(near[0]).start
+            push(half, blocks, at, len(near) * BLOCK, *near_slot(half, blocks))
+
+    def class_blocks(part):
+        return [part + CLASSES * at for at in range(members)]
+
+    def far_slot(half, part):
+        return far_weights.at[half * CLASSES + part], far_low.at[half * CLASSES + part]
+
+    def push_far(half, part):
+        push(half, class_blocks(part), part * class_rows, span, *far_slot(half, part))
 
     def put(kind, src, dst, from_rows, to_rows, block):
         @pl.when(me == block)
@@ -497,37 +551,49 @@
     dv_acc[...] = jnp.zeros_like(dv_acc)
     dq_acc[...] = jnp.zeros_like(dq_acc)
 
+    def put_queries(half, part):
+        rows = rows_of(half, class_blocks(part))
+        dq_low[rows, :] = (dq_acc[:, rows] * scale).T.astype(jnp.bfloat16)
+        for block in class_blocks(part):
+            put(Q_OUT + half, dq_low, dq_out, query_rows(half, block), half_rows(half), block)
+
+    def put_keys(part):
+        own = pl.ds(part * span, class_rows)
+        dk_low[own, :] = (dk_acc[own, :] * scale).astype(jnp.bfloat16)
+        for block in class_blocks(part):
+            put(K_OUT, dk_low, dk_out, key_rows(block), all_rows, block)
+        dv_low[own, :] = dv_acc[own, :].astype(jnp.bfloat16)
+        for block in class_blocks(part):
+            put(V_OUT, dv_low, dv_out, key_rows(block), all_rows, block)
+
     loads[2].wait()
     loads[3].wait()
     arrived(K_IN, k_all, key_rows)
     kt_all[...] = k_all[...].T
-    arrived(V_IN, v_all, key_rows)
-    for index in range(peers):
-        place = stat_all.at[index]
-        pltpu.make_async_copy(place, place, in_recv.at[S_IN, index]).wait()
-
-    pair = 2
+    tiles_arrived(NORM_IN, norm_all)
     for half in range(HALVES):
         arrived(Q_IN + half, q_all, places[half])
+        for part in range(CLASSES):
+            weigh(
+                half, class_blocks(part), part * class_rows, span, None, *far_slot(half, part)
+            )
+            for blocks in pairs(part):
+                weigh_near(half, blocks)
+    arrived(V_IN, v_all, key_rows)
+    tiles_arrived(DELTA_IN, delta_all)
+
+    for half in range(HALVES):
         arrived(G_IN + half, g_all, places[half])
-        for part in range(CLASSES):
-            for at in range(0, members, pair):
-                visit_near(half, [part + CLASSES * (at + step) for step in range(pair)])
-        for part in range(CLASSES):
-            blocks = [part + CLASSES * at for at in range(members)]
-            visit(half, blocks, part * class_rows, span, None)
-            rows = pl.ds(query_rows(half, part).start, members * HALF)
-            dq_low[rows, :] = (dq_acc[:, rows] * scale).T.astype(jnp.bfloat16)
-            for block in blocks:
-                put(Q_OUT + half, dq_low, dq_out, query_rows(half, block), half_rows(half), block)
-            if half == HALVES - 1:
-                own = pl.ds(part * span, class_rows)
-                dk_low[own, :] = (dk_acc[own, :] * scale).astype(jnp.bfloat16)
-                for block in blocks:
-                    put(K_OUT, dk_low, dk_out, key_rows(block), all_rows, block)
-                dv_low[own, :] = dv_acc[own, :].astype(jnp.bfloat16)
-                for block in blocks:
-                    put(V_OUT, dv_low, dv_out, key_rows(block), all_rows, block)
+        push_near(half, 1)
+        push_far(half, 0)
+        if half == HALVES - 1:
+            put_keys(0)
+        push_near(half, 0)
+        put_queries(half, 0)
+        push_far(half, 1)
+        if half == HALVES - 1:
+            put_keys(1)
+        put_queries(half, 1)
 
     middle = pl.ds(class_rows, GLOB)
     glob_low[0] = (dk_acc[middle, :] * scale).astype(jnp.bfloat16)
@@ -624,6 +690,9 @@
     tokens = peers * BLOCK
     low, full = jnp.bfloat16, jnp.float32
     head_peers = lax.axis_size("head")
+    members = peers // CLASSES
+    far = (HALVES * CLASSES, members * BLOCK + GLOB, members * HALF)
+    near = (HALVES * peers // PAIR, (PAIR + 1) * BLOCK, PAIR * HALF)
     result = jax.ShapeDtypeStruct((row_count, col_count), low)
     scores = tokens * (GLOB + (RAND + 3) * BLOCK)
     dq, dk, dv, glob = pl.pallas_call(
@@ -650,11 +719,17 @@
             pltpu.VMEM((tokens + GLOB, HEAD_DIM), low),
             pltpu.VMEM((tokens, HEAD_DIM), low),
             pltpu.VMEM((peers, 8, BLOCK), full),
+            pltpu.VMEM((peers, 8, BLOCK), full),
             pltpu.VMEM((row_count, col_count), low),
             pltpu.VMEM((row_count, col_count), low),
             pltpu.VMEM(log_norm.shape, full),
             pltpu.VMEM((peers, 8, BLOCK), full),
+            pltpu.VMEM((peers, 8, BLOCK), full),
             pltpu.VMEM((HEAD_DIM, tokens + GLOB), low),
+            pltpu.VMEM(far, full),
+            pltpu.VMEM(far, low),
+            pltpu.VMEM(near, full),
+            pltpu.VMEM(near, low),
             pltpu.VMEM((HEAD_DIM, tokens), full),
             pltpu.VMEM((tokens + GLOB, HEAD_DIM), full),
             pltpu.VMEM((tokens + GLOB, HEAD_DIM), full),

time: 56.6 us -> 58 us (1.025)
  Pallas kernels: 55.8 us -> 57.2 us
    pallas_call x1, Pallas kernels: 53.9 us -> 55.3 us  [whole_heads(): pl.pallas_call(functools.partial(head_kernel, peers), out_shape=(result,...]
where the time goes in v1:
time: 58 us; the launch traced here: 57.9 us
  Pallas kernels  57.2 us (99%)
  between operations  0.64 us (1%)
    pallas_call x1, Pallas kernels, whole_heads(): pl.pallas_call(functools.partial(head_kernel, peers), out_shape=(result,...  55.3 us
    pallas_call x1, Pallas kernels, whole_heads(): pl.pallas_call(finish_kernel, out_shape=(result, result, result, share, s...  1.97 us

profile of v1, /device:TPU:0, one launch (start us, length us, event | category | flops | bytes accessed | tf_op | source)
XLA Modules:
  0.0 57.9 jit_solution(4502041843004573450)
XLA Ops:
  0.6 55.3 %whole_heads.1 = (bf16[128,1024]{1,0:T(8,128)(2,1)}, bf16[128,1024]{1,0:T(8,128)(2,1)}, bf16[128,1024]{1,0:T(8,128)(2,1)}, bf16[2,32,1024]{2,1,0:T(8,128)(2,1)}) custom-call(bf16[128,1024]{1,0:T(8,128)(2,1)} %q_hbm.1, bf16[128,1024]{1,0:T(8,128)(2,1)} %k_hbm.1, bf16[128,1024]{1,0:T(8,128)(2,1)} %v_hbm.1, bf16[128,1024]{1,0:T(8,128)(2,1)} %o_hbm.1, ...), custom_call_target="tpu_custom_call" | custom-call | flops 1342177280 | bytes 4194304 | tf_op jit(solution)/shard_map/whole_heads/pallas_call | solution.py:698
  55.9 2.0 %finish.1 = (bf16[128,1024]{1,0:T(8,128)(2,1)}, bf16[128,1024]{1,0:T(8,128)(2,1)}, bf16[128,1024]{1,0:T(8,128)(2,1)}, f32[32,1024]{1,0:T(8,128)}, f32[32,1024]{1,0:T(8,128)}) custom-call(bf16[128,1024]{1,0:T(8,128)(2,1)} %get-tuple-element.9.dq_in, bf16[128,1024]{1,0:T(8,128)(2,1)} %get-tuple-element.10.dk_in, bf16[128,1024]{1,0:T(8,128)(2,1)} %get-tuple-element.11.dv_in, ...), custom_call_target="tpu_custom_call" | custom-call | bytes 2097152 | tf_op jit(solution)/shard_map/finish/pallas_call | solution.py:758

commit v2 on v0

--- a/solution.py
+++ b/solution.py
@@ -263,6 +263,7 @@
     o_own,
     norm_own,
     stat_own,
+    g_tiles,
     kt_all,
     dq_acc,
     dk_acc,
@@ -272,6 +273,8 @@
     dv_low,
     glob_low,
     load_sem,
+    tile_sem,
+    store_sem,
     spread_send,
     spread_recv,
     in_send,
@@ -324,16 +327,23 @@
             gv_hbm.at[:, cols(me)], v_all.at[pl.ds(class_rows, GLOB)], load_sem.at[3]
         ),
     ]
-    firsts = [
-        pltpu.make_async_copy(src, dst, load_sem.at[4 + at])
-        for at, (src, dst) in enumerate(
-            ((g_hbm, g_part), (k_hbm, k_own), (q_hbm, q_own), (v_hbm, v_own))
-        )
-    ]
-    for load in firsts:
-        load.start()
     for load in loads:
         load.start()
+    spread_load = pltpu.make_async_copy(g_hbm, g_part, load_sem.at[4])
+    spread_load.start()
+
+    def tile_loads(at, src, dst):
+        copies = [
+            pltpu.make_async_copy(src.at[:, cols(index)], dst.at[index], tile_sem.at[at, index])
+            for index in range(peers)
+        ]
+        for copy in copies:
+            copy.start()
+        return copies
+
+    k_loads = tile_loads(0, k_hbm, k_own)
+    q_loads = tile_loads(1, q_hbm, q_own)
+    v_loads = tile_loads(2, v_hbm, v_own)
 
     barrier = pltpu.get_barrier_semaphore()
     for by in range(1, head_peers):
@@ -353,7 +363,7 @@
     pl.semaphore_wait(barrier, head_peers - 1 + peers - 1)
 
     sends = []
-    firsts[0].wait()
+    spread_load.wait()
 
     def my_part():
         return pl.ds(pl.multiple_of(my_head * part_rows, part_rows), part_rows)
@@ -380,7 +390,7 @@
         for by in order:
             to = lax.rem(me + by, peers)
             copy = remote(
-                src.at[from_rows, cols(to)],
+                src.at[to, from_rows],
                 dst.at[rows(me)],
                 in_send.at[kind, by],
                 in_recv.at[kind, me],
@@ -389,7 +399,7 @@
             copy.start()
             sends.append(copy)
         pltpu.make_async_copy(
-            src.at[from_rows, cols(me)], dst.at[rows(me)], in_recv.at[kind, me]
+            src.at[me, from_rows], dst.at[rows(me)], in_recv.at[kind, me]
         ).start()
 
     def arrived(kind, dst, rows):
@@ -399,11 +409,14 @@
 
     places = [functools.partial(query_rows, half) for half in range(HALVES)]
     all_rows = pl.ds(0, BLOCK)
-    firsts[1].wait()
+    for load in k_loads:
+        load.wait()
     spread_in(K_IN, k_own, k_all, all_rows, key_rows)
-    firsts[2].wait()
+    for load in q_loads:
+        load.wait()
     spread_in(Q_IN, q_own, q_all, half_rows(0), places[0])
-    firsts[3].wait()
+    for load in v_loads:
+        load.wait()
     spread_in(V_IN, v_own, v_all, all_rows, key_rows)
 
     loads[0].wait()
@@ -411,7 +424,9 @@
     for index in range(head_peers):
         place = g_own.at[pl.ds(index * part_rows, part_rows)]
         pltpu.make_async_copy(place, place, spread_recv.at[index]).wait()
-    spread_in(G_IN, g_own, g_all, half_rows(0), places[0])
+    for index in range(peers):
+        g_tiles[index] = g_own[:, pl.ds(index * HEAD_DIM, HEAD_DIM)]
+    spread_in(G_IN, g_tiles, g_all, half_rows(0), places[0])
     ones = jnp.ones((8, HEAD_DIM), jnp.float32)
     first = lax.broadcasted_iota(jnp.int32, (8, BLOCK), 0) == 0
     for index in range(peers):
@@ -437,7 +452,7 @@
 
     for half in range(1, HALVES):
         spread_in(Q_IN + half, q_own, q_all, half_rows(half), places[half])
-        spread_in(G_IN + half, g_own, g_all, half_rows(half), places[half])
+        spread_in(G_IN + half, g_tiles, g_all, half_rows(half), places[half])
 
     scale = HEAD_DIM**-0.5
 
@@ -480,14 +495,14 @@
         @pl.when(me == block)
         def _():
             pltpu.make_async_copy(
-                src.at[from_rows], dst.at[to_rows, cols(me)], out_recv.at[kind, me]
+                src.at[from_rows], dst.at[me, to_rows], out_recv.at[kind, me]
             ).start()
 
         @pl.when(me != block)
         def _():
             remote(
                 src.at[from_rows],
-                dst.at[to_rows, cols(me)],
+                dst.at[me, to_rows],
                 out_send.at[kind, block],
                 out_recv.at[kind, me],
                 ctx=block,
@@ -540,7 +555,7 @@
         to = lax.rem(me + by, peers)
         copy = remote(
             share_of(to),
-            glob_out.at[:, :, cols(me)],
+            glob_out.at[me],
             out_send.at[GLOB_OUT, to],
             out_recv.at[GLOB_OUT, me],
             ctx=to,
@@ -548,30 +563,31 @@
         copy.start()
         sends.append(copy)
     pltpu.make_async_copy(
-        share_of(me), glob_out.at[:, :, cols(me)], out_recv.at[GLOB_OUT, me]
+        share_of(me), glob_out.at[me], out_recv.at[GLOB_OUT, me]
     ).start()
 
     stores = []
 
-    def store(at, src, dst):
-        copy = pltpu.make_async_copy(src, dst, load_sem.at[8 + at])
-        copy.start()
-        stores.append(copy)
+    def land(kind, src, dst):
+        for index in range(peers):
+            place = src(index)
+            pltpu.make_async_copy(place, place, out_recv.at[kind, index]).wait()
+            copy = pltpu.make_async_copy(place, dst(index), store_sem.at[kind, index])
+            copy.start()
+            stores.append(copy)
+
+    def land_rows(kind, src, dst, rows):
+        land(kind, lambda index: src.at[index, rows], lambda index: dst.at[rows, cols(index)])
 
     for half in range(HALVES):
-        for index in range(peers):
-            place = dq_out.at[half_rows(half), cols(index)]
-            pltpu.make_async_copy(place, place, out_recv.at[Q_OUT + half, index]).wait()
-    store(0, dq_out, dq_hbm)
-    for at, (kind, dst, home) in enumerate(((K_OUT, dk_out, dk_hbm), (V_OUT, dv_out, dv_hbm))):
-        for index in range(peers):
-            place = dst.at[:, cols(index)]
-            pltpu.make_async_copy(place, place, out_recv.at[kind, index]).wait()
-        store(1 + at, dst, home)
-    for index in range(peers):
-        place = glob_out.at[:, :, cols(index)]
-        pltpu.make_async_copy(place, place, out_recv.at[GLOB_OUT, index]).wait()
-    store(3, glob_out, glob_hbm)
+        land_rows(Q_OUT + half, dq_out, dq_hbm, half_rows(half))
+    land_rows(K_OUT, dk_out, dk_hbm, all_rows)
+    land_rows(V_OUT, dv_out, dv_hbm, all_rows)
+    land(
+        GLOB_OUT,
+        lambda index: glob_out.at[index],
+        lambda index: glob_hbm.at[:, :, cols(index)],
+    )
 
     for copy in sends:
         copy.wait_send()
@@ -624,6 +640,7 @@
     tokens = peers * BLOCK
     low, full = jnp.bfloat16, jnp.float32
     head_peers = lax.axis_size("head")
+    tiles = (peers, row_count, HEAD_DIM)
     result = jax.ShapeDtypeStruct((row_count, col_count), low)
     scores = tokens * (GLOB + (RAND + 3) * BLOCK)
     dq, dk, dv, glob = pl.pallas_call(
@@ -637,14 +654,14 @@
         in_specs=[pl.BlockSpec(memory_space=pl.ANY)] * 8,
         out_specs=[pl.BlockSpec(memory_space=pl.ANY)] * 4,
         scratch_shapes=[
-            pltpu.VMEM((row_count, col_count), low),
-            pltpu.VMEM((row_count, col_count), low),
-            pltpu.VMEM((row_count, col_count), low),
+            pltpu.VMEM(tiles, low),
+            pltpu.VMEM(tiles, low),
+            pltpu.VMEM(tiles, low),
             pltpu.VMEM(grad_out.shape, low),
-            pltpu.VMEM((row_count, col_count), low),
-            pltpu.VMEM((row_count, col_count), low),
-            pltpu.VMEM((row_count, col_count), low),
-            pltpu.VMEM((2, GLOB // peers, col_count), low),
+            pltpu.VMEM(tiles, low),
+            pltpu.VMEM(tiles, low),
+            pltpu.VMEM(tiles, low),
+            pltpu.VMEM((peers, 2, GLOB // peers, HEAD_DIM), low),
             pltpu.VMEM((tokens, HEAD_DIM), low),
             pltpu.VMEM((tokens + GLOB, HEAD_DIM), low),
             pltpu.VMEM((tokens + GLOB, HEAD_DIM), low),
@@ -654,6 +671,7 @@
             pltpu.VMEM((row_count, col_count), low),
             pltpu.VMEM(log_norm.shape, full),
             pltpu.VMEM((peers, 8, BLOCK), full),
+            pltpu.VMEM(tiles, low),
             pltpu.VMEM((HEAD_DIM, tokens + GLOB), low),
             pltpu.VMEM((HEAD_DIM, tokens), full),
             pltpu.VMEM((tokens + GLOB, HEAD_DIM), full),
@@ -662,7 +680,9 @@
             pltpu.VMEM((tokens + GLOB, HEAD_DIM), low),
             pltpu.VMEM((tokens + GLOB, HEAD_DIM), low),
             pltpu.VMEM((2, GLOB, HEAD_DIM), low),
-            pltpu.SemaphoreType.DMA((12,)),
+            pltpu.SemaphoreType.DMA((5,)),
+            pltpu.SemaphoreType.DMA((3, peers)),
+            pltpu.SemaphoreType.DMA((OUT_KINDS, peers)),
             pltpu.SemaphoreType.DMA((head_peers,)),
             pltpu.SemaphoreType.DMA((head_peers,)),
             pltpu.SemaphoreType.DMA((IN_KINDS, peers)),

time: 56.6 us -> 57.1 us (level)
  no operation moved by 1% of the time
where the time goes in v2:
time: 57.1 us; the launch traced here: 57 us
  Pallas kernels  56.3 us (99%)
  between operations  0.64 us (1%)
    pallas_call x1, Pallas kernels, whole_heads(): pl.pallas_call(functools.partial(head_kernel, peers), out_shape=(result,...  54.4 us
    pallas_call x1, Pallas kernels, whole_heads(): pl.pallas_call(finish_kernel, out_shape=(result, result, result, share, s...  1.97 us

profile of v2, /device:TPU:0, one launch (start us, length us, event | category | flops | bytes accessed | tf_op | source)
XLA Modules:
  0.0 57.0 jit_solution(2417941676336783730)
XLA Ops:
  0.6 54.4 %whole_heads.1 = (bf16[128,1024]{1,0:T(8,128)(2,1)}, bf16[128,1024]{1,0:T(8,128)(2,1)}, bf16[128,1024]{1,0:T(8,128)(2,1)}, bf16[2,32,1024]{2,1,0:T(8,128)(2,1)}) custom-call(bf16[128,1024]{1,0:T(8,128)(2,1)} %q_hbm.1, bf16[128,1024]{1,0:T(8,128)(2,1)} %k_hbm.1, bf16[128,1024]{1,0:T(8,128)(2,1)} %v_hbm.1, bf16[128,1024]{1,0:T(8,128)(2,1)} %o_hbm.1, ...), custom_call_target="tpu_custom_call" | custom-call | flops 1342177280 | bytes 4194304 | tf_op jit(solution)/shard_map/whole_heads/pallas_call | solution.py:646
  55.0 2.0 %finish.1 = (bf16[128,1024]{1,0:T(8,128)(2,1)}, bf16[128,1024]{1,0:T(8,128)(2,1)}, bf16[128,1024]{1,0:T(8,128)(2,1)}, f32[32,1024]{1,0:T(8,128)}, f32[32,1024]{1,0:T(8,128)}) custom-call(bf16[128,1024]{1,0:T(8,128)(2,1)} %get-tuple-element.9.dq_in, bf16[128,1024]{1,0:T(8,128)(2,1)} %get-tuple-element.10.dk_in, bf16[128,1024]{1,0:T(8,128)(2,1)} %get-tuple-element.11.dv_in, ...), custom_call_target="tpu_custom_call" | custom-call | bytes 2097152 | tf_op jit(solution)/shard_map/finish/pallas_call | solution.py:703

commit v3 on v0

--- a/solution.py
+++ b/solution.py
@@ -217,7 +217,7 @@
     )
 
 
-HALVES = 2
+HALVES = 1
 HALF = BLOCK // HALVES
 K_IN, V_IN, S_IN, Q_IN, G_IN = 0, 1, 2, 3, 3 + HALVES
 IN_KINDS = 3 + 2 * HALVES

time: 56.6 us -> 59.1 us (1.044)
  Pallas kernels: 55.8 us -> 58.3 us
    pallas_call x1, Pallas kernels: 53.9 us -> 56.3 us  [whole_heads(): pl.pallas_call(functools.partial(head_kernel, peers), out_shape=(result,...]
where the time goes in v3:
time: 59.1 us; the launch traced here: 59 us
  Pallas kernels  58.3 us (99%)
  between operations  0.64 us (1%)
    pallas_call x1, Pallas kernels, whole_heads(): pl.pallas_call(functools.partial(head_kernel, peers), out_shape=(result,...  56.3 us
    pallas_call x1, Pallas kernels, whole_heads(): pl.pallas_call(finish_kernel, out_shape=(result, result, result, share, s...  1.97 us

profile of v3, /device:TPU:0, one launch (start us, length us, event | category | flops | bytes accessed | tf_op | source)
XLA Modules:
  0.0 59.0 jit_solution(3375117536506238391)
XLA Ops:
  0.6 56.3 %whole_heads.1 = (bf16[128,1024]{1,0:T(8,128)(2,1)}, bf16[128,1024]{1,0:T(8,128)(2,1)}, bf16[128,1024]{1,0:T(8,128)(2,1)}, bf16[2,32,1024]{2,1,0:T(8,128)(2,1)}) custom-call(bf16[128,1024]{1,0:T(8,128)(2,1)} %q_hbm.1, bf16[128,1024]{1,0:T(8,128)(2,1)} %k_hbm.1, bf16[128,1024]{1,0:T(8,128)(2,1)} %v_hbm.1, bf16[128,1024]{1,0:T(8,128)(2,1)} %o_hbm.1, ...), custom_call_target="tpu_custom_call" | custom-call | flops 1342177280 | bytes 4194304 | tf_op jit(solution)/shard_map/whole_heads/pallas_call | solution.py:629
  57.0 2.0 %finish.1 = (bf16[128,1024]{1,0:T(8,128)(2,1)}, bf16[128,1024]{1,0:T(8,128)(2,1)}, bf16[128,1024]{1,0:T(8,128)(2,1)}, f32[32,1024]{1,0:T(8,128)}, f32[32,1024]{1,0:T(8,128)}) custom-call(bf16[128,1024]{1,0:T(8,128)(2,1)} %get-tuple-element.9.dq_in, bf16[128,1024]{1,0:T(8,128)(2,1)} %get-tuple-element.10.dk_in, bf16[128,1024]{1,0:T(8,128)(2,1)} %get-tuple-element.11.dv_in, ...), custom_call_target="tpu_custom_call" | custom-call | bytes 2097152 | tf_op jit(solution)/shard_map/finish/pallas_call | solution.py:683
